TPU v7x, 512 devices: a whole 4x4x16 slice. The times are simulated.
512 devices in a mesh: dp: 4 (over z_lo), ctx: 16 (over y, x), tp: 8 (over z_hi, core).
Axes of the slice: x: 4, y: 4, z: 16 (z_hi: 4, z_lo: 4; z = z_hi * 4 + z_lo), core: 2. Of those that a mesh axis runs over, the one named last changes fastest.
Arguments:
- query_b: bfloat16 [8192, 8192], P(('dp', 'ctx'), 'tp'), parts along dimension 0, may hold values from -6 to 6
- key_b: bfloat16 [8192, 8192], P(('dp', 'ctx'), 'tp'), parts along dimension 0, may hold values from -6 to 6
- value_b: bfloat16 [8192, 8192], P(('dp', 'ctx'), 'tp'), parts along dimension 0, may hold values from -6 to 6
- filter_b: bfloat16 [2048, 8192], P('ctx', 'tp'), may hold values from -6 to 6
- skip_b: bfloat16 [8192], P('tp'), may hold values from 0.5 to 1.5
- acts_a: bfloat16 [2048, 8192], P(('dp', 'tp'), 'ctx'), parts along dimension 0, may hold values from -1800 to 1800
- gain_a: float32 [8192], P('ctx'), may hold values from 0.1 to 1.9
- w_gate: bfloat16 [8192, 11264], P('ctx', 'tp'), may hold values from -0.0625 to 0.0625
- w_up: bfloat16 [8192, 11264], P('ctx', 'tp'), may hold values from -0.0625 to 0.0625
- grad_hidden: bfloat16 [2048, 11264], P(('dp', 'ctx'), 'tp'), parts along dimension 0, may hold values from -6 to 6
Outputs:
- gated: bfloat16 [8192, 8192], P(('dp', 'ctx'), 'tp'), parts along dimension 0
- grad_gate: bfloat16 [2048, 11264], P(('dp', 'ctx'), 'tp'), parts along dimension 0
- grad_up: bfloat16 [2048, 11264], P(('dp', 'ctx'), 'tp'), parts along dimension 0
There are 4 independent parts, one for each index of `dp`. A program takes and returns all parts, laid end to end along the dimension named above; an argument that names none is the same for every part. Nothing has to cross between parts.
All inputs are finite; a program needn't handle non-finite values.
Results may differ from a plain program's by a relative error of at most 0.0053.
Values may be sent and summed in bfloat16 or wider, within the bound.
A program may use at most 64 MiB of HBM per device.

v0:
```python
import math

import jax
import jax.numpy as jnp
from jax import lax
from jax.sharding import PartitionSpec as P

D = 8192


transform_precision = lax.Precision.HIGH
epsilon = 1e-06


def tables(height, breadth, period):
    row_index = jnp.arange(height, dtype=jnp.int32)[:, None]
    col_index = jnp.arange(breadth, dtype=jnp.int32)[None, :]
    phases = (row_index * col_index % period).astype(jnp.float32) * (2.0 * math.pi / period)
    return (jnp.cos(phases), jnp.sin(phases))


def product(form, left, right):
    return jnp.einsum(form, left, right, precision=transform_precision)


def causal_filter(signal, taps, blocks):
    length, breadth = signal.shape
    period = 2 * length
    outer = 2 * blocks
    inner = length // blocks
    cos_small, sin_small = tables(outer, blocks, outer)
    cos_twist, sin_twist = tables(outer, inner, period)
    cos_large, sin_large = tables(inner, inner, inner)
    twist_cos = cos_twist[:, :, None]
    twist_sin = sin_twist[:, :, None]

    def forward(values):
        shaped = values.reshape(blocks, inner, breadth)
        first_re = product("kn,nqc->kqc", cos_small, shaped)
        first_im = -product("kn,nqc->kqc", sin_small, shaped)
        turned_re = first_re * twist_cos + first_im * twist_sin
        turned_im = first_im * twist_cos - first_re * twist_sin
        spec_re = product("pq,kqc->pkc", cos_large, turned_re) + product(
            "pq,kqc->pkc", sin_large, turned_im
        )
        spec_im = product("pq,kqc->pkc", cos_large, turned_im) - product(
            "pq,kqc->pkc", sin_large, turned_re
        )
        return (spec_re, spec_im)

    signal_re, signal_im = forward(signal)
    taps_re, taps_im = forward(taps)
    joint_re = signal_re * taps_re - signal_im * taps_im
    joint_im = signal_re * taps_im + signal_im * taps_re
    back_re = product("pq,pkc->qkc", cos_large, joint_re) - product(
        "pq,pkc->qkc", sin_large, joint_im
    )
    back_im = product("pq,pkc->qkc", cos_large, joint_im) + product(
        "pq,pkc->qkc", sin_large, joint_re
    )
    untwist_cos = cos_twist.T[:, :, None]
    untwist_sin = sin_twist.T[:, :, None]
    final_re = back_re * untwist_cos - back_im * untwist_sin
    final_im = back_im * untwist_cos + back_re * untwist_sin
    result = product("kn,qkc->nqc", cos_small, final_re) - product(
        "kn,qkc->nqc", sin_small, final_im
    )
    return result.reshape(length, breadth) / period


def mixer_part(query_b, key_b, value_b, filter_b, skip_b):
    seq_rows, local_width = key_b.shape
    group = lax.axis_size("ctx")
    block_width = local_width // group
    mixed = (key_b.astype(jnp.float32) * value_b.astype(jnp.float32)).astype(jnp.bfloat16)
    mixed_sectioned = mixed.reshape(seq_rows, group, block_width)
    taps_sectioned = filter_b.reshape(seq_rows, group, block_width)
    query_sectioned = query_b.reshape(seq_rows, group, block_width)
    skip_sectioned = skip_b.reshape(1, group, block_width)
    mixed_seq = lax.all_to_all(mixed_sectioned, "ctx", split_axis=1, concat_axis=0, tiled=True)
    taps_seq = lax.all_to_all(taps_sectioned, "ctx", split_axis=1, concat_axis=0, tiled=True)
    query_seq = lax.all_to_all(query_sectioned, "ctx", split_axis=1, concat_axis=0, tiled=True)
    skip_seq = lax.all_to_all(skip_sectioned, "ctx", split_axis=1, concat_axis=0, tiled=True)
    breadth = mixed_seq.shape[2]
    signal = mixed_seq.reshape(-1, breadth).astype(jnp.float32)
    conv = causal_filter(signal, taps_seq.reshape(-1, breadth).astype(jnp.float32), group)
    conv = lax.optimization_barrier(conv.astype(jnp.bfloat16)).astype(jnp.float32)
    direct = skip_seq[0, 0].astype(jnp.float32)[None, :] * signal
    result = (query_seq.reshape(-1, breadth).astype(jnp.float32) * (conv + direct)).astype(
        jnp.bfloat16
    )
    returned = lax.all_to_all(
        result.reshape(-1, 1, breadth), "ctx", split_axis=0, concat_axis=1, tiled=True
    )
    return returned.reshape(seq_rows, local_width)


def mlp_part(acts_a, gain_a, w_gate, w_up, grad_hidden):
    gathered = lax.all_gather(acts_a, "tp", axis=0, tiled=True)
    rows_f32 = gathered.astype(jnp.float32)
    squares = lax.psum(jnp.sum(rows_f32 * rows_f32, axis=1), "ctx")
    scaling = lax.rsqrt(squares / D + epsilon)
    normed = (rows_f32 * scaling[:, None] * gain_a[None, :]).astype(jnp.bfloat16)
    hidden_width = w_gate.shape[1]
    gate_term = jnp.dot(normed, w_gate, preferred_element_type=jnp.float32)
    up_term = jnp.dot(normed, w_up, preferred_element_type=jnp.float32)
    summed = lax.psum_scatter(
        jnp.concatenate((gate_term, up_term), axis=1), "ctx", scatter_dimension=0, tiled=True
    )
    gate = summed[:, :hidden_width]
    up_part = summed[:, hidden_width:]
    sigma = jax.nn.sigmoid(gate)
    upstream = grad_hidden.astype(jnp.float32)
    grad_gate = (upstream * up_part * sigma * (1.0 + gate * (1.0 - sigma))).astype(jnp.bfloat16)
    grad_up = (upstream * gate * sigma).astype(jnp.bfloat16)
    return (grad_gate, grad_up)


def body(query_b, key_b, value_b, filter_b, skip_b, acts_a, gain_a, w_gate, w_up, grad_hidden):
    gated = mixer_part(query_b, key_b, value_b, filter_b, skip_b)
    grad_gate, grad_up = mlp_part(acts_a, gain_a, w_gate, w_up, grad_hidden)
    return (gated, grad_gate, grad_up)


def solution(mesh):
    return jax.shard_map(
        body,
        mesh=mesh,
        in_specs=(
            P(("dp", "ctx"), "tp"),
            P(("dp", "ctx"), "tp"),
            P(("dp", "ctx"), "tp"),
            P("ctx", "tp"),
            P("tp"),
            P(("dp", "tp"), "ctx"),
            P("ctx"),
            P("ctx", "tp"),
            P("ctx", "tp"),
            P(("dp", "ctx"), "tp"),
        ),
        out_specs=(P(("dp", "ctx"), "tp"), P(("dp", "ctx"), "tp"), P(("dp", "ctx"), "tp")),
        check_vma=False,
    )
```

profile of v0, /device:TPU:1, one launch (start us, length us, event | category | flops | bytes accessed | tf_op | source)
XLA Modules:
  0.0 180.9 jit_solution(3873166049479830671)
XLA Ops:
  7.2 29.5 %all_gather.3 = bf16[512,512]{1,0:T(8,128)(2,1)S(1)} all-gather(bf16[64,512]{1,0:T(8,128)(2,1)} %param.15), channel_id=1, replica_groups=mesh['dp'=4,'ctx'=16,'tp'=8] {'tp'}, dimensions={0}, use_global_device_ids=true | all-gather | bytes 589824 | tf_op jit(solution)/shard_map/all_gather | solution.py:99
  36.9 33.5 %psum.7 = f32[512]{0:T(512)S(1)} all-reduce(f32[512]{0:T(512)S(1)} %fusion.2), channel_id=1, replica_groups=mesh['dp'=4,'ctx'=16,'tp'=8] {'ctx'}, use_global_device_ids=true, to_apply=%region_1.2 | all-reduce | flops 512 | bytes 4096 | tf_op jit(solution)/shard_map/psum | solution.py:101
  70.4 1.8 %fusion.27 = f32[512,1408]{1,0:T(8,128)S(1)} fusion(bf16[512,1408]{1,0:T(8,128)(2,1)S(1)} %copy-done, bf16[512,512]{1,0:T(8,128)(2,1)S(1)} %all_gather.3, f32[512]{0:T(512)} %param.16, f32[512]{0:T(512)S(1)} %add_rsqrt_fusion), kind=kOutput, calls=%fused_computation.49 | convolution fusion | flops 739246080 | bytes 4853760 | tf_op jit(solution)/shard_map/dot_general | solution.py:106
  72.2 1.0 fusion.29
  73.3 2.9 %pad_maximum_fusion = f32[512,2816]{1,0:T(8,128)} fusion(f32[512,1408]{1,0:T(8,128)S(1)} %fusion.27, f32[512,1408]{1,0:T(8,128)S(1)} %fusion.29), kind=kLoop, calls=%fused_computation | loop fusion | flops 1441792 | bytes 11534336 | tf_op jit(solution)/shard_map/concatenate | solution.py:108
  77.6 3.5 %all-to-all-start.3 = ((bf16[1,16,64]{2,0,1:T(2,128)(2,1)}), bf16[1,16,64]{2,0,1:T(2,128)(2,1)S(1)}, u32[]{:S(2)}, u32[]{:S(2)}) async-start(bf16[1,16,64]{2,0,1:T(2,128)(2,1)} %reshape.172), calls=%async_computation.3 | async-start | bytes 16384 | tf_op jit(solution)/shard_map/all_to_all | solution.py:83
  82.9 0.8 copy.89
  83.7 3.6 %all-to-all-done.3 = bf16[1,16,64]{2,0,1:T(2,128)(2,1)S(1)} async-done(((bf16[1,16,64]{2,0,1:T(2,128)(2,1)}), bf16[1,16,64]{2,0,1:T(2,128)(2,1)S(1)}, u32[]{:S(2)}, u32[]{:S(2)}) %all-to-all-start.3) | async-done | bytes 2080 | tf_op jit(solution)/shard_map/all_to_all | solution.py:83
  87.3 3.5 %all-to-all-start.2 = ((bf16[128,16,64]{0,2,1:T(8,128)(2,1)}), bf16[128,16,64]{0,2,1:T(8,128)(2,1)S(1)}, u32[]{:S(2)}, u32[]{:S(2)}) async-start(bf16[128,16,64]{0,2,1:T(8,128)(2,1)} %bitcast.17), calls=%async_computation.2 | async-start | bytes 524288 | tf_op jit(solution)/shard_map/all_to_all | solution.py:81
  93.0 7.2 %all-to-all-done.2 = bf16[128,16,64]{0,2,1:T(8,128)(2,1)S(1)} async-done(((bf16[128,16,64]{0,2,1:T(8,128)(2,1)}), bf16[128,16,64]{0,2,1:T(8,128)(2,1)S(1)}, u32[]{:S(2)}, u32[]{:S(2)}) %all-to-all-start.2) | async-done | bytes 262176 | tf_op jit(solution)/shard_map/all_to_all | solution.py:81
  100.1 4.2 %all-to-all-start.1 = ((bf16[128,16,64]{0,2,1:T(8,128)(2,1)}), bf16[128,16,64]{0,2,1:T(8,128)(2,1)}, u32[]{:S(2)}, u32[]{:S(2)}) async-start(bf16[128,16,64]{0,2,1:T(8,128)(2,1)} %bitcast.4), calls=%async_computation.1 | async-start | bytes 524288 | tf_op jit(solution)/shard_map/all_to_all | solution.py:80
  104.9 1.5 fusion.13
  106.4 6.9 %all-to-all-done.1 = bf16[128,16,64]{0,2,1:T(8,128)(2,1)} async-done(((bf16[128,16,64]{0,2,1:T(8,128)(2,1)}), bf16[128,16,64]{0,2,1:T(8,128)(2,1)}, u32[]{:S(2)}, u32[]{:S(2)}) %all-to-all-start.1) | async-done | bytes 262176 | tf_op jit(solution)/shard_map/all_to_all | solution.py:80
  113.3 4.4 %all-to-all-start = ((bf16[128,16,64]{0,2,1:T(8,128)(2,1)}), bf16[128,16,64]{0,2,1:T(8,128)(2,1)}, u32[]{:S(2)}, u32[]{:S(2)}) async-start(bf16[128,16,64]{0,2,1:T(8,128)(2,1)} %bitcast.170), calls=%async_computation | async-start | bytes 524288 | tf_op jit(solution)/shard_map/all_to_all | solution.py:82
  117.7 1.5 fusion.16
  119.1 1.9 %multiply_add_fusion.3 = (f32[32,128,64]{1,0,2:T(8,128)S(1)}, f32[32,128,64]{1,0,2:T(8,128)S(1)}, f32[32,128,64]{1,0,2:T(8,128)S(1)}, f32[32,128,64]{1,0,2:T(8,128)S(1)}) fusion(f32[32,128,64]{1,0,2:T(8,128)S(1)} %fusion.16, f32[32,128]{1,0:T(8,128)} %get-tuple-element.27, f32[32,128]{1,0:T(8,128)} %get-tuple-element.28, f32[32,128,64]{1,0,2:T(8,128)S(1)} %fusion.13, ...), kind=kOutput, calls=%fused_computation.21 | convolution fusion | flops 28580864 | bytes 7634944 | tf_op jit(solution)/shard_map/kn,nqc->kqc/dot_general | solution.py:23
  123.5 0.8 fusion.61
  125.2 0.8 fusion.49
  126.9 0.8 fusion.59
  130.2 1.2 multiply_subtract_fusion.1
  131.4 1.1 fusion.53
  132.5 0.8 fusion.39
  133.4 0.8 fusion.41
  134.2 0.8 fusion.51
  135.8 0.9 fusion.6
  136.7 0.9 fusion.1
  137.7 1.0 convert_bitcast_fusion
  139.1 1.1 bitcast_convert_fusion
  142.6 13.7 %all_to_all.66 = bf16[16,2,4096]{2,1,0:T(2,128)(2,1)S(1)} all-to-all(bf16[16,2,4096]{2,1,0:T(2,128)(2,1)S(1)} %reshape.173), channel_id=1, replica_groups=mesh['dp'=4,'ctx'=16,'tp'=8] {'ctx'}, dimensions={0} | all-to-all | bytes 524288 | tf_op jit(solution)/shard_map/all_to_all | solution.py:92
  157.6 0.9 copy.103
  158.5 13.7 %reduce-scatter.2.cloned.1.call-done = f32[32,2816]{1,0:T(8,128)} async-done(((f32[512,2816]{1,0:T(8,128)}), f32[32,2816]{1,0:T(8,128)}) %reduce-scatter.2.cloned.1.call-update) | async-done | bytes 360464 | tf_op jit(solution)/shard_map/reduce_scatter | solution.py:107
  172.2 1.8 fusion.26
  (60 shorter events, 17.5 us)
Async XLA Ops:
  7.2 63.2 %copy-start = (bf16[512,1408]{1,0:T(8,128)(2,1)S(1)}, bf16[512,1408]{1,0:T(8,128)(2,1)}, u32[]{:S(2)}) copy-start(bf16[512,1408]{1,0:T(8,128)(2,1)} %param.18) | copy-start | bytes 4325380
  7.2 165.1 %reduce-scatter.2.cloned.1.call-start = ((), (), s32[]{:S(2)}) async-start(), calls=%async_computation.6 | async-start | bytes 6127616 | tf_op jit(solution)/shard_map/reduce_scatter | solution.py:107
  70.4 1.8 %copy-start.2 = (bf16[512,1408]{1,0:T(8,128)(2,1)S(1)}, bf16[512,1408]{1,0:T(8,128)(2,1)}, u32[]{:S(2)}) copy-start(bf16[512,1408]{1,0:T(8,128)(2,1)} %param.17) | copy-start | bytes 4325380
  70.4 1.8 %copy-start.9 = (f32[512]{0:T(512)S(1)}, f32[512]{0:T(512)}, u32[]{:S(2)}) copy-start(f32[512]{0:T(512)} %param.16) | copy-start | bytes 6148
  76.2 0.7 copy-start.10
  76.2 4.8 %copy-start.3 = (bf16[128,1024]{1,0:T(8,128)(2,1)S(1)}, bf16[128,1024]{1,0:T(8,128)(2,1)}, u32[]{:S(2)}) copy-start(bf16[128,1024]{1,0:T(8,128)(2,1)} %param.11) | copy-start | bytes 786436
  76.2 5.0 %copy-start.4 = (bf16[128,1024]{1,0:T(8,128)(2,1)S(1)}, bf16[128,1024]{1,0:T(8,128)(2,1)}, u32[]{:S(2)}) copy-start(bf16[128,1024]{1,0:T(8,128)(2,1)} %param.12) | copy-start | bytes 786436
  76.2 6.7 %copy-start.5 = (bf16[128,1024]{1,0:T(8,128)(2,1)S(1)}, bf16[128,1024]{1,0:T(8,128)(2,1)}, u32[]{:S(2)}) copy-start(bf16[128,1024]{1,0:T(8,128)(2,1)} %param.13) | copy-start | bytes 786436
  76.9 14.7 %copy-start.6 = (bf16[128,1024]{1,0:T(8,128)(2,1)S(1)}, bf16[128,1024]{1,0:T(8,128)(2,1)}, u32[]{:S(2)}) copy-start(bf16[128,1024]{1,0:T(8,128)(2,1)} %param.10) | copy-start | bytes 786436
  77.6 9.7 %all-to-all-start.3 = ((bf16[1,16,64]{2,0,1:T(2,128)(2,1)}), bf16[1,16,64]{2,0,1:T(2,128)(2,1)S(1)}, u32[]{:S(2)}, u32[]{:S(2)}) async-start(bf16[1,16,64]{2,0,1:T(2,128)(2,1)} %reshape.172), calls=%async_computation.3 | async-start | bytes 16384 | tf_op jit(solution)/shard_map/all_to_all | solution.py:83
  87.3 12.8 %all-to-all-start.2 = ((bf16[128,16,64]{0,2,1:T(8,128)(2,1)}), bf16[128,16,64]{0,2,1:T(8,128)(2,1)S(1)}, u32[]{:S(2)}, u32[]{:S(2)}) async-start(bf16[128,16,64]{0,2,1:T(8,128)(2,1)} %bitcast.17), calls=%async_computation.2 | async-start | bytes 524288 | tf_op jit(solution)/shard_map/all_to_all | solution.py:81
  100.1 4.2 %copy-start.1 = (bf16[128,16,64]{0,2,1:T(8,128)(2,1)}, bf16[128,16,64]{0,2,1:T(8,128)(2,1)S(1)}, u32[]{:S(2)}) copy-start(bf16[128,16,64]{0,2,1:T(8,128)(2,1)S(1)} %all-to-all-done.2) | copy-start | bytes 786436
  100.1 13.1 %all-to-all-start.1 = ((bf16[128,16,64]{0,2,1:T(8,128)(2,1)}), bf16[128,16,64]{0,2,1:T(8,128)(2,1)}, u32[]{:S(2)}, u32[]{:S(2)}) async-start(bf16[128,16,64]{0,2,1:T(8,128)(2,1)} %bitcast.4), calls=%async_computation.1 | async-start | bytes 524288 | tf_op jit(solution)/shard_map/all_to_all | solution.py:80
  113.3 24.5 %all-to-all-start = ((bf16[128,16,64]{0,2,1:T(8,128)(2,1)}), bf16[128,16,64]{0,2,1:T(8,128)(2,1)}, u32[]{:S(2)}, u32[]{:S(2)}) async-start(bf16[128,16,64]{0,2,1:T(8,128)(2,1)} %bitcast.170), calls=%async_computation | async-start | bytes 524288 | tf_op jit(solution)/shard_map/all_to_all | solution.py:82
  132.5 2.5 %copy-start.8 = (f32[128,32]{0,1:T(8,128)S(1)}, f32[128,32]{0,1:T(8,128)}, u32[]{:S(2)}) copy-start(f32[128,32]{0,1:T(8,128)} %get-tuple-element.30) | copy-start | bytes 49156
  136.7 3.5 %copy-start.11 = (f32[64]{0:T(128)S(1)}, f32[64]{0:T(128)}, u32[]{:S(2)}) copy-start(f32[64]{0:T(128)} %fusion.99) | copy-start | bytes 772
  142.2 30.1 %copy-start.7 = (bf16[32,1408]{1,0:T(8,128)(2,1)S(1)}, bf16[32,1408]{1,0:T(8,128)(2,1)}, u32[]{:S(2)}) copy-start(bf16[32,1408]{1,0:T(8,128)(2,1)} %param.19) | copy-start | bytes 270340
Sparse Core Ops, SparseCore 0:
  76.4 95.8 reduce-scatter.1
where the time goes:
time: 182 us; the launch traced here: 181 us
  blocking collectives  76.7 us (42%)
  waiting for transfers between devices  31.4 us (17%)
  matrix products  20.3 us (11%)
  starting transfers between devices  15.6 us (9%)
  between operations  14.5 us (8%)
  other arithmetic  12.8 us (7%)
  local copies, waits for them, and re-layouts  9.58 us (5%)
    psum x1, blocking collectives, mlp_part(): squares = lax.psum(jnp.sum(rows_f32 * rows_f32, axis=1), 'ctx')  33.5 us
    all_gather x1, blocking collectives, mlp_part(): gathered = lax.all_gather(acts_a, 'tp', axis=0, tiled=True)  29.5 us
    reduce_scatter x1, waiting for transfers between devices, mlp_part(): lax.psum_scatter(jnp.concatenate((gate_term, up_term), axis=1), 'ctx', sc...  13.7 us
    all_to_all x1, blocking collectives, mixer_part(): lax.all_to_all(result.reshape(-1, 1, breadth), 'ctx', split_axis=0, conca...  13.7 us
    unnamed x12, matrix products  10.2 us
    dot_general x6, matrix products, product(): return jnp.einsum(form, left, right, precision=transform_precision)  7.29 us
    all_to_all x1, waiting for transfers between devices, mixer_part(): lax.all_to_all(taps_sectioned, 'ctx', split_axis=1, concat_axis=0, tiled=...  7.16 us
    all_to_all x1, waiting for transfers between devices, mixer_part(): lax.all_to_all(mixed_sectioned, 'ctx', split_axis=1, concat_axis=0, tiled...  6.88 us
  transfers between devices with their start and end apart: 5, of which 4 were waited for; matrix products, arithmetic and copies ran while one was open for 19% of the time, Pallas kernels for 0%

commit v1 on v0

v1 whole, which is shorter than its diff:
```python
import functools
import math

import jax
import jax.numpy as jnp
import numpy as np
from jax import lax
from jax.experimental import pallas as pl
from jax.experimental.pallas import tpu as pltpu
from jax.sharding import PartitionSpec as P

D = 8192
EPSILON = 1e-06
SIDE = 4
GROUP = 16
BLOCK = 256
CHUNKS = (384, 384, 384, 256)
STARTS = tuple(sum(CHUNKS[:i]) for i in range(len(CHUNKS)))
MESH = pl.DeviceIdType.MESH
F32 = jnp.float32
BF16 = jnp.bfloat16


def dft_tables():
    order = np.concatenate((np.arange(0, BLOCK, 2), np.arange(1, BLOCK, 2)))
    angle = np.outer(2 * order + 1, np.arange(BLOCK)) % (4 * BLOCK)
    angle = angle.astype(np.float64) * (math.pi / (2 * BLOCK))
    full = np.concatenate((np.cos(angle), -np.sin(angle)), axis=0)
    high = full.astype(jnp.bfloat16)
    low = (full - high.astype(np.float64)).astype(jnp.bfloat16)
    back = np.ascontiguousarray((full.T / BLOCK)).astype(jnp.bfloat16)
    return high, low, back


def kernel(
    query_h, key_h, value_h, taps_h, skip_ref, acts_h, gain_ref, wg_h, wu_h, grad_h,
    high_h, low_h, back_h,
    gated_ref, gg_ref, gu_ref,
    query, key, value, taps, wg, wu, grad, high, low, back,
    mixed, send_u, recv_u, spec, turned, joint, send_c, recv_c,
    rows, scaled, send_q, recv_q, spread,
    *rest,
):
    n = len(CHUNKS)
    parts = (rest[0:n], rest[n:2 * n])
    got1p, got1m, got2p, got2m, sums, got3p, got3m, got4p, got4m = (
        (rest[(2 + 2 * i) * n:(3 + 2 * i) * n], rest[(3 + 2 * i) * n:(4 + 2 * i) * n])
        for i in range(9)
    )
    (load_sem, u_send, u_recv, c_send, c_recv, q_send, q_recv, z_send, z_recv,
     r_send, r_recv) = rest[20 * n:]

    ctx = lax.axis_index("ctx")
    tp = lax.axis_index("tp")
    y, x = lax.div(ctx, SIDE), lax.rem(ctx, SIDE)
    z, core = lax.div(tp, 2), lax.rem(tp, 2)

    def turn(value_, by):
        return lax.rem(value_ + by, SIDE)

    left = turn(z, 3) * 2 + core
    right = turn(z, 1) * 2 + core
    far = turn(z, 2) * 2 + core
    other = z * 2 + 1 - core

    loads = {}
    for i, (name, src, dst) in enumerate((
        ("key", key_h, key), ("value", value_h, value), ("taps", taps_h, taps),
        ("acts", acts_h, rows.at[tp]), ("high", high_h, high), ("low", low_h, low),
        ("wg", wg_h, wg), ("wu", wu_h, wu), ("back", back_h, back),
        ("query", query_h, query), ("grad", grad_h, grad),
    )):
        loads[name] = pltpu.make_async_copy(src, dst, load_sem.at[i])
        loads[name].start()

    barrier = pltpu.get_barrier_semaphore()

    @pl.loop(1, GROUP)
    def _(k):
        pl.semaphore_signal(
            barrier, inc=1, device_id={"ctx": lax.rem(ctx + k, GROUP)}, device_id_type=MESH)

    for peer in (left, right, other):
        pl.semaphore_signal(barrier, inc=1, device_id={"tp": peer}, device_id_type=MESH)

    lane = lax.broadcasted_iota(jnp.int32, (128, 128), 1)
    low_half = lane < 64

    for name in ("key", "value", "taps"):
        loads[name].wait()

    @pl.loop(0, GROUP // 2)
    def _(i):
        at = pl.ds(pl.multiple_of(i * 128, 128), 128)
        signal = (key[:, at].astype(F32) * value[:, at].astype(F32)).astype(BF16)
        mixed[:, at] = signal
        signal = signal.astype(F32)
        lags = taps[:, at].astype(F32)
        send_u[2 * i] = jnp.where(low_half, signal, pltpu.roll(lags, 64, 1)).astype(BF16)
        send_u[2 * i + 1] = jnp.where(low_half, pltpu.roll(signal, 64, 1), lags).astype(BF16)

    pl.semaphore_wait(barrier, GROUP + 2)

    def z_copy(i, block, half, peer, whole=False):
        at = rows.at[block] if whole else rows.at[block, pl.ds(32 * half, 32)]
        return pltpu.make_async_remote_copy(
            src_ref=at, dst_ref=at, send_sem=z_send.at[i], recv_sem=z_recv.at[i],
            device_id={"tp": peer}, device_id_type=MESH)

    loads["acts"].wait()
    own = [
        z_copy(0, tp, 0, right), z_copy(1, tp, 1, left),
        z_copy(2, tp, 1, right), z_copy(3, tp, 0, left),
        z_copy(4, tp, 0, other, whole=True),
    ]
    for copy in own:
        copy.start()

    def exchange(src, dst, send_sem, recv_sem, pick=lambda peer: peer):
        def one(k):
            peer = lax.rem(ctx + k, GROUP)
            return pltpu.make_async_remote_copy(
                src_ref=src.at[pick(peer)], dst_ref=dst.at[ctx],
                send_sem=send_sem.at[peer], recv_sem=recv_sem.at[ctx],
                device_id={"ctx": peer}, device_id_type=MESH)

        def arrival(k):
            peer = lax.rem(ctx + k, GROUP)
            return pltpu.make_async_remote_copy(
                src_ref=src.at[pick(peer)], dst_ref=dst.at[peer],
                send_sem=send_sem.at[peer], recv_sem=recv_sem.at[peer],
                device_id={"ctx": peer}, device_id_type=MESH)

        def start():
            @pl.loop(1, GROUP)
            def _(k):
                one(k).start()

        def wait_recv():
            @pl.loop(1, GROUP)
            def _(k):
                arrival(k).wait_recv()

        def wait_send():
            @pl.loop(1, GROUP)
            def _(k):
                one(k).wait_send()

        return start, wait_recv, wait_send

    u_start, u_wait, u_drain = exchange(send_u, recv_u, u_send, u_recv)
    c_start, c_wait, c_drain = exchange(send_c, recv_c, c_send, c_recv)
    q_start, q_wait, q_drain = exchange(
        send_q, recv_q, q_send, q_recv, lambda peer: lax.div(peer, SIDE))
    u_start()
    recv_u[ctx] = send_u[ctx]

    z_copy(0, left, 0, right).wait_recv()
    ahead = z_copy(5, left, 0, right)
    ahead.start()
    z_copy(1, right, 1, left).wait_recv()
    behind = z_copy(6, right, 1, left)
    behind.start()
    passed = [z_copy(7, left, 0, other), z_copy(8, right, 1, other)]
    passed[0].start()
    passed[1].start()
    z_copy(2, left, 1, right).wait_recv()
    passed.append(z_copy(9, left, 1, other))
    passed[2].start()
    z_copy(3, right, 0, left).wait_recv()
    passed.append(z_copy(10, right, 0, other))
    passed[3].start()

    u_wait()
    loads["high"].wait()
    loads["low"].wait()

    @pl.loop(0, 4)
    def _(i):
        pair = jnp.concatenate(
            (recv_u[pl.ds(4 * i, 2)].reshape(BLOCK, 128),
             recv_u[pl.ds(4 * i + 2, 2)].reshape(BLOCK, 128)), axis=1)
        result = jnp.dot(high[...], pair, preferred_element_type=F32)
        result += jnp.dot(low[...], pair, preferred_element_type=F32)
        for h in range(2):
            half = result[:, 128 * h:128 * h + 128]
            spec[2 * i + h] = half
            turned[2 * i + h] = pltpu.roll(half, 64, 1)

    @pl.loop(0, 16)
    def _(r):
        re = pl.ds(pl.multiple_of(16 * r, 16), 16)
        im = pl.ds(pl.multiple_of(BLOCK + 16 * r, 16), 16)
        sign = 1.0 - 2.0 * lax.div(r, 8).astype(F32)
        last = None
        for i in range(8):
            total_re = total_im = None
            for a in range(i // 2 + 1):
                b = i - a
                a_re, a_im = spec[a, re], spec[a, im]
                b_re, b_im = turned[b, re], turned[b, im]
                one_re = a_re * b_re - a_im * b_im
                one_im = a_re * b_im + a_im * b_re
                if a == b:
                    one_re, one_im = 0.5 * one_re, 0.5 * one_im
                total_re = one_re if total_re is None else total_re + one_re
                total_im = one_im if total_im is None else total_im + one_im
            if last is None:
                joint[i, re] = total_re.astype(BF16)
                joint[i, im] = total_im.astype(BF16)
            else:
                joint[i, re] = (total_re - sign * last[1]).astype(BF16)
                joint[i, im] = (total_im + sign * last[0]).astype(BF16)
            last = (total_re, total_im)

    loads["back"].wait()

    @pl.loop(0, 4)
    def _(i):
        pair = jnp.concatenate((joint[2 * i], joint[2 * i + 1]), axis=1)
        result = jnp.dot(back[...], pair, preferred_element_type=F32)
        for h in range(2):
            half = result[:, 128 * h:128 * h + 128]
            half = half + pltpu.roll(half, 64, 1)
            for d in range(2):
                send_c[4 * i + 2 * h + d] = jnp.where(
                    low_half[:64], half[128 * d:128 * d + 64], half[128 * d + 64:128 * d + 128]
                ).astype(BF16)

    c_start()
    recv_c[ctx] = send_c[ctx]

    z_copy(5, far, 0, right).wait_recv()
    passed.append(z_copy(11, far, 0, other))
    passed[4].start()
    z_copy(6, far, 1, left).wait_recv()
    passed.append(z_copy(12, far, 1, other))
    passed[5].start()
    mate = 1 - core
    z_copy(4, other, 0, other, whole=True).wait_recv()
    for i, block, half in (
        (7, turn(z, 3), 0), (8, turn(z, 1), 1), (9, turn(z, 3), 1), (10, turn(z, 1), 0),
        (11, turn(z, 2), 0), (12, turn(z, 2), 1),
    ):
        z_copy(i, block * 2 + mate, half, other).wait_recv()

    @pl.loop(0, SIDE)
    def _(i):
        block = rows[pl.ds(2 * i, 2)].reshape(128, 512).astype(F32)
        squares = block * block
        squares = (squares[:, :128] + squares[:, 128:256]) + (
            squares[:, 256:384] + squares[:, 384:])
        send_q[i] = jnp.broadcast_to(
            jnp.sum(squares.T, axis=0, keepdims=True), (8, 128))
        scaled[pl.ds(pl.multiple_of(128 * i, 128), 128)] = (
            block * gain_ref[...]).astype(BF16)

    q_start()
    recv_q[ctx] = send_q[y]

    first = (x, y)
    second = (y, x)

    def place(g, step, by):
        along_x = (g == 0) == (step == 0)
        return turn(x, by) + SIDE * y if along_x else x + SIDE * turn(y, by)

    def r_copy(g, c, kind, src, dst, by):
        i = (g * n + c) * 8 + kind
        return pltpu.make_async_remote_copy(
            src_ref=src, dst_ref=dst, send_sem=r_send.at[i], recv_sem=r_recv.at[i],
            device_id={"ctx": place(g, 0 if kind < 4 else 1, by)}, device_id_type=MESH)

    def link(g, c, kind):
        part, f, s = parts[g][c], first[g], second[g]
        total = sums[g][c]
        if kind == 0:
            return r_copy(g, c, 0, part.at[turn(f, 2), pl.ds(0, 2)], got1p[g][c], 1)
        if kind == 1:
            return r_copy(g, c, 1, part.at[turn(f, 2), pl.ds(2, 2)], got1m[g][c], 3)
        if kind == 2:
            return r_copy(g, c, 2, part.at[turn(f, 1)], got2p[g][c], 1)
        if kind == 3:
            return r_copy(g, c, 3, part.at[turn(f, 3)], got2m[g][c], 3)
        if kind == 4:
            return r_copy(g, c, 4, total.at[turn(s, 2), pl.ds(0, 16)], got3p[g][c], 1)
        if kind == 5:
            return r_copy(g, c, 5, total.at[turn(s, 2), pl.ds(16, 16)], got3m[g][c], 3)
        if kind == 6:
            return r_copy(g, c, 6, total.at[turn(s, 1)], got4p[g][c], 1)
        return r_copy(g, c, 7, total.at[turn(s, 3)], got4m[g][c], 3)

    weights = (wg, wu)
    loads["wg"].wait()
    loads["wu"].wait()

    def step1(g, c):
        width = CHUNKS[c]
        part = parts[g][c]

        @pl.loop(0, 2)
        def _(i):
            result = jnp.dot(
                scaled[pl.ds(pl.multiple_of(256 * i, 256), 256)],
                weights[g][:, STARTS[c]:STARTS[c] + width], preferred_element_type=F32)
            for b in range(8):
                block = result[32 * b:32 * b + 32].astype(BF16)
                row, col = 2 * i + b // 4, b % 4
                if g == 0:
                    part[col, row] = block
                else:
                    part[row, col] = block

        link(g, c, 0).start()
        link(g, c, 1).start()

    def add(into, index, value_):
        into[index] = (into[index].astype(F32) + value_.astype(F32)).astype(BF16)

    def step2(g, c):
        part, f = parts[g][c], first[g]
        link(g, c, 0).wait_recv()
        for b in range(2):
            add(part, (turn(f, 1), b), got1p[g][c][b])
        link(g, c, 2).start()
        link(g, c, 1).wait_recv()
        for b in range(2):
            add(part, (turn(f, 3), 2 + b), got1m[g][c][b])
        link(g, c, 3).start()

    def step3(g, c):
        part, f = parts[g][c], first[g]
        link(g, c, 2).wait_recv()
        link(g, c, 3).wait_recv()
        for b in range(SIDE):
            sums[g][c][b] = (
                part[f, b].astype(F32) + got2p[g][c][b].astype(F32)
                + got2m[g][c][b].astype(F32)).astype(BF16)
        link(g, c, 4).start()
        link(g, c, 5).start()

    def step4(g, c):
        total, s = sums[g][c], second[g]
        link(g, c, 4).wait_recv()
        add(total, (turn(s, 1), pl.ds(0, 16)), got3p[g][c][...])
        link(g, c, 6).start()
        link(g, c, 5).wait_recv()
        add(total, (turn(s, 3), pl.ds(16, 16)), got3m[g][c][...])
        link(g, c, 7).start()

    def finish(c, scale):
        values = []
        for g in range(2):
            link(g, c, 6).wait_recv()
            link(g, c, 7).wait_recv()
            total = (sums[g][c][second[g]].astype(F32) + got4p[g][c][...].astype(F32)
                     + got4m[g][c][...].astype(F32))
            values.append(total * scale)
        gate, up = values
        at = slice(STARTS[c], STARTS[c] + CHUNKS[c])
        sigma = jax.nn.sigmoid(gate)
        upstream = grad[:, at].astype(F32)
        gg_ref[:, at] = (upstream * up * sigma * (1.0 + gate * (1.0 - sigma))).astype(BF16)
        gu_ref[:, at] = (upstream * gate * sigma).astype(BF16)

    for c in range(n):
        for g in range(2):
            step1(g, c)

    for c in range(n + 2):
        if c < n:
            step2(0, c)
            step2(1, c)
        if 0 <= c - 1 < n:
            step3(0, c - 1)
            step3(1, c - 1)
        if 0 <= c - 2 < n:
            step4(0, c - 2)
            step4(1, c - 2)
        if c == 1:
            c_wait()
            loads["query"].wait()

            @pl.loop(0, GROUP // 2)
            def _(i):
                at = pl.ds(pl.multiple_of(i * 128, 128), 128)
                even = recv_c[2 * i].astype(F32)
                odd = recv_c[2 * i + 1].astype(F32)
                conv = jnp.concatenate(
                    (jnp.where(low_half[:64], even, pltpu.roll(odd, 64, 1)),
                     jnp.where(low_half[:64], pltpu.roll(even, 64, 1), odd)), axis=0)
                direct = skip_ref[:, at].astype(F32) * mixed[:, at].astype(F32)
                gated_ref[:, at] = (
                    query[:, at].astype(F32) * (conv + direct)).astype(BF16)

    q_wait()
    power = recv_q[0]
    for i in range(1, GROUP):
        power = power + recv_q[i]
    spread[...] = jnp.broadcast_to(power[0:1], (128, 128)).T
    mine = spread[pl.ds(pl.multiple_of(32 * x, 32), 32), :]
    scale = lax.rsqrt(mine[:, :1] / D + EPSILON)
    loads["grad"].wait()
    for c in range(n):
        finish(c, scale)

    u_drain()
    c_drain()
    q_drain()
    for copy in own + [ahead, behind] + passed:
        copy.wait_send()
    for g in range(2):
        for c in range(n):
            for kind in range(8):
                link(g, c, kind).wait_send()


def body(query_b, key_b, value_b, filter_b, skip_b, acts_a, gain_a, w_gate, w_up, grad_hidden):
    high, low, back = dft_tables()
    any_spec = pl.BlockSpec(memory_space=pl.ANY)
    vmem = pl.BlockSpec(memory_space=pltpu.VMEM)
    length, width = key_b.shape
    hidden = w_gate.shape[1]

    def per_chunk(*lead):
        return [pltpu.VMEM(lead + (w,), BF16) for w in CHUNKS] * 2

    scratch = [
        pltpu.VMEM((length, width), BF16),
        pltpu.VMEM((length, width), BF16),
        pltpu.VMEM((length, width), BF16),
        pltpu.VMEM((length, width), BF16),
        pltpu.VMEM(w_gate.shape, BF16),
        pltpu.VMEM(w_up.shape, BF16),
        pltpu.VMEM(grad_hidden.shape, BF16),
        pltpu.VMEM(high.shape, BF16),
        pltpu.VMEM(low.shape, BF16),
        pltpu.VMEM(back.shape, BF16),
        pltpu.VMEM((length, width), BF16),
        pltpu.VMEM((GROUP, 128, 128), BF16),
        pltpu.VMEM((GROUP, 128, 128), BF16),
        pltpu.VMEM((8, 2 * BLOCK, 128), F32),
        pltpu.VMEM((8, 2 * BLOCK, 128), F32),
        pltpu.VMEM((8, 2 * BLOCK, 128), BF16),
        pltpu.VMEM((GROUP, 64, 128), BF16),
        pltpu.VMEM((GROUP, 64, 128), BF16),
        pltpu.VMEM((8, 64, 512), BF16),
        pltpu.VMEM((512, 512), BF16),
        pltpu.VMEM((SIDE, 8, 128), F32),
        pltpu.VMEM((GROUP, 8, 128), F32),
        pltpu.VMEM((128, 128), F32),
    ]
    scratch += per_chunk(SIDE, SIDE, 32)
    scratch += per_chunk(2, 32) + per_chunk(2, 32)
    scratch += per_chunk(SIDE, 32) + per_chunk(SIDE, 32)
    scratch += per_chunk(SIDE, 32)
    scratch += per_chunk(16) + per_chunk(16)
    scratch += per_chunk(32) + per_chunk(32)
    links = 2 * len(CHUNKS) * 8
    for size in (11, GROUP, GROUP, GROUP, GROUP, GROUP, GROUP, 13, 13, links, links):
        scratch.append(pltpu.SemaphoreType.DMA((size,)))
    return pl.pallas_call(
        kernel,
        out_shape=(
            jax.ShapeDtypeStruct((length, width), BF16),
            jax.ShapeDtypeStruct(grad_hidden.shape, BF16),
            jax.ShapeDtypeStruct(grad_hidden.shape, BF16),
        ),
        in_specs=[any_spec] * 4 + [vmem, any_spec, vmem] + [any_spec] * 6,
        out_specs=(vmem, vmem, vmem),
        scratch_shapes=scratch,
        compiler_params=pltpu.CompilerParams(
            collective_id=0, has_side_effects=True, vmem_limit_bytes=56 * 1024 * 1024),
        name="hyena",
    )(
        query_b, key_b, value_b, filter_b, skip_b.reshape(1, -1), acts_a,
        gain_a.reshape(1, -1), w_gate, w_up, grad_hidden,
        jnp.asarray(high), jnp.asarray(low), jnp.asarray(back),
    )


def solution(mesh):
    return jax.shard_map(
        body,
        mesh=mesh,
        in_specs=(
            P(("dp", "ctx"), "tp"),
            P(("dp", "ctx"), "tp"),
            P(("dp", "ctx"), "tp"),
            P("ctx", "tp"),
            P("tp"),
            P(("dp", "tp"), "ctx"),
            P("ctx"),
            P("ctx", "tp"),
            P("ctx", "tp"),
            P(("dp", "ctx"), "tp"),
        ),
        out_specs=(P(("dp", "ctx"), "tp"), P(("dp", "ctx"), "tp"), P(("dp", "ctx"), "tp")),
        check_vma=False,
    )
```

time: 182 us -> 65.3 us (0.36)
  blocking collectives: 76.7 us -> 0 us
  Pallas kernels: 0 us -> 58.3 us
  waiting for transfers between devices: 31.4 us -> 0 us
  matrix products: 20.3 us -> 0 us
  starting transfers between devices: 15.6 us -> 0 us
  between operations: 14.5 us -> 0.64 us
  other arithmetic: 12.8 us -> 0 us
  local copies, waits for them, and re-layouts: 9.58 us -> 6.02 us
    pallas_call x0 -> x1, Pallas kernels: none -> 58.3 us  [body(): pl.pallas_call(kernel, out_shape=(jax.ShapeDtypeStruct((length, width), B...]
    psum x1 -> x0, blocking collectives: 33.5 us -> none  [mlp_part(): squares = lax.psum(jnp.sum(rows_f32 * rows_f32, axis=1), 'ctx')]
    all_gather x1 -> x0, blocking collectives: 29.5 us -> none  [mlp_part(): gathered = lax.all_gather(acts_a, 'tp', axis=0, tiled=True)]
    all_to_all x4 -> x0, waiting for transfers between devices: 17.6 us -> none  [the longest x1 7.16 us: mixer_part(): lax.all_to_all(taps_sectioned, 'ctx', split_axis=1, concat_axis=0, tiled=...]
    all_to_all x4 -> x0, starting transfers between devices: 15.6 us -> none  [the longest x1 4.37 us: mixer_part(): lax.all_to_all(query_sectioned, 'ctx', split_axis=1, concat_axis=0, tiled...]
    reduce_scatter x1 -> x0, waiting for transfers between devices: 13.7 us -> none  [mlp_part(): lax.psum_scatter(jnp.concatenate((gate_term, up_term), axis=1), 'ctx', sc...]
    all_to_all x1 -> x0, blocking collectives: 13.7 us -> none  [mixer_part(): lax.all_to_all(result.reshape(-1, 1, breadth), 'ctx', split_axis=0, conca...]
    unnamed x12 -> x0, matrix products: 10.2 us -> none
  transfers between devices with their start and end apart: 5 -> 0, of which waited for: 4 -> 0; matrix products, arithmetic and copies ran while one was open for 19% -> 0% of each run, Pallas kernels for 0% -> 0%
where the time goes in v1:
time: 65.3 us; the launch traced here: 65 us
  Pallas kernels  58.3 us (89%)
  local copies, waits for them, and re-layouts  6.02 us (9%)
    pallas_call x1, Pallas kernels, body(): pl.pallas_call(kernel, out_shape=(jax.ShapeDtypeStruct((length, width), B...  58.3 us
    unnamed x3, local copies, waits for them, and re-layouts  4.74 us

profile of v1, /device:TPU:1, one launch (start us, length us, event | category | flops | bytes accessed | tf_op | source)
XLA Modules:
  0.0 65.0 jit_solution(9135915321525606149)
XLA Ops:
  0.6 1.3 %reshape.12.skip_ref = bf16[1,1024]{1,0:T(2,128)(2,1)} reshape(bf16[1024]{0:T(1024)(128)(2,1)} %param.17) | data formatting | bytes 4096 | tf_op jit(solution)/shard_map/reshape | solution.py:476
  1.9 58.3 %hyena.1 = (bf16[128,1024]{1,0:T(8,128)(2,1)}, bf16[32,1408]{1,0:T(8,128)(2,1)}, bf16[32,1408]{1,0:T(8,128)(2,1)}) custom-call(bf16[128,1024]{1,0:T(8,128)(2,1)} %query_h.1, bf16[128,1024]{1,0:T(8,128)(2,1)} %key_h.1, bf16[128,1024]{1,0:T(8,128)(2,1)} %value_h.1, bf16[128,1024]{1,0:T(8,128)(2,1)} %taps_h.1, bf16[1,1024]{1,0:T(2,128)(2,1)} %reshape.12.skip_ref, ...), custom_call_target="tpu_custom_call" | custom-call | tf_op jit(solution)/shard_map/hyena/pallas_call | solution.py:462
  60.3 1.7 %copy.19 = bf16[128,1024]{1,0:T(8,128)(2,1)} copy(bf16[128,1024]{1,0:T(8,128)(2,1)} %get-tuple-element.6) | data formatting | bytes 524288
  61.9 1.5 %copy.20 = bf16[32,1408]{1,0:T(8,128)(2,1)} copy(bf16[32,1408]{1,0:T(8,128)(2,1)} %get-tuple-element.7) | data formatting | bytes 180224
  63.5 1.5 %copy.21 = bf16[32,1408]{1,0:T(8,128)(2,1)} copy(bf16[32,1408]{1,0:T(8,128)(2,1)} %get-tuple-element.8) | data formatting | bytes 180224

commit v2 on v0

v2 whole, which is shorter than its diff:
```python
import math

import jax
import jax.numpy as jnp
import numpy as np
from jax import lax
from jax.experimental import pallas as pl
from jax.experimental.pallas import tpu as pltpu
from jax.sharding import PartitionSpec as P

D = 8192
EPSILON = 1e-06
SIDE = 4
GROUP = 16
BLOCK = 256
CHUNKS = (384, 384, 384, 256)
STARTS = tuple(sum(CHUNKS[:i]) for i in range(len(CHUNKS)))
MESH = pl.DeviceIdType.MESH
F32 = jnp.float32
BF16 = jnp.bfloat16


def dft_tables():
    order = np.concatenate((np.arange(0, BLOCK, 2), np.arange(1, BLOCK, 2)))
    angle = np.outer(2 * order + 1, np.arange(BLOCK)) % (4 * BLOCK)
    angle = angle.astype(np.float64) * (math.pi / (2 * BLOCK))
    full = np.concatenate((np.cos(angle), -np.sin(angle)), axis=0)
    high = full.astype(jnp.bfloat16)
    low = (full - high.astype(np.float64)).astype(jnp.bfloat16)
    back = np.ascontiguousarray((full.T / BLOCK)).astype(jnp.bfloat16)
    return high, low, back


def kernel(
    query_h, key_h, value_h, taps_h, skip_ref, acts_h, gain_ref, wg_h, wu_h,
    high_h, low_h, back_h,
    gated_ref, gate_ref, up_ref,
    query, key, value, taps, wg, wu, high, low, back,
    mixed, send_u, recv_u, spec, turned, joint, send_c, recv_c,
    rows, scaled, send_q, recv_q, spread,
    *rest,
):
    n = len(CHUNKS)
    (parts, s1_out, s1p_in, s1m_in, s2p_out, s2m_out, s2p_in, s2m_in,
     t1_out, t1p_in, t1m_in, t2p_out, t2m_out, t2p_in, t2m_in) = (
        (rest[2 * i * n:(2 * i + 1) * n], rest[(2 * i + 1) * n:(2 * i + 2) * n])
        for i in range(15)
    )
    t0_in = rest[30 * n:30 * n + 2]
    (load_sem, u_send, u_recv, c_send, c_recv, q_send, q_recv, z_send, z_recv,
     r_send, r_recv) = rest[30 * n + 2:]

    ctx = lax.axis_index("ctx")
    tp = lax.axis_index("tp")
    y, x = lax.div(ctx, SIDE), lax.rem(ctx, SIDE)
    z, core = lax.div(tp, 2), lax.rem(tp, 2)

    def turn(value_, by):
        return lax.rem(value_ + by, SIDE)

    left = turn(z, 3) * 2 + core
    right = turn(z, 1) * 2 + core
    far = turn(z, 2) * 2 + core
    other = z * 2 + 1 - core
    left_mate, right_mate = turn(z, 3) * 2 + 1 - core, turn(z, 1) * 2 + 1 - core

    barrier = pltpu.get_barrier_semaphore()

    @pl.loop(1, GROUP)
    def _(k):
        pl.semaphore_signal(
            barrier, inc=1, device_id={"ctx": lax.rem(ctx + k, GROUP)}, device_id_type=MESH)

    for peer in (left, right, other, left_mate, right_mate):
        pl.semaphore_signal(barrier, inc=1, device_id={"tp": peer}, device_id_type=MESH)

    loads = {}
    for i, (name, src, dst) in enumerate((
        ("key", key_h, key), ("value", value_h, value), ("taps", taps_h, taps),
        ("acts", acts_h, rows.at[tp]), ("high", high_h, high), ("low", low_h, low),
        ("wg", wg_h, wg), ("wu", wu_h, wu), ("back", back_h, back),
        ("query", query_h, query),
    )):
        loads[name] = pltpu.make_async_copy(src, dst, load_sem.at[i])
        loads[name].start()

    lane = lax.broadcasted_iota(jnp.int32, (128, 128), 1)
    low_half = lane < 64

    pl.semaphore_wait(barrier, GROUP + 4)

    def z_copy(i, block, half, peer, whole=False, first=False):
        part = pl.ds(0, 64) if whole else pl.ds(32 * half, 32)
        at = rows.at[block, part]
        return pltpu.make_async_remote_copy(
            src_ref=acts_h.at[part] if first else at, dst_ref=at,
            send_sem=z_send.at[i], recv_sem=z_recv.at[i],
            device_id={"tp": peer}, device_id_type=MESH)

    own = [
        z_copy(0, tp, 0, right, first=True), z_copy(1, tp, 1, left, first=True),
        z_copy(4, tp, 0, other, whole=True, first=True),
        z_copy(2, tp, 1, right, first=True), z_copy(3, tp, 0, left, first=True),
    ]
    for copy in own[:3]:
        copy.start()

    for name in ("key", "value", "taps"):
        loads[name].wait()

    @pl.loop(0, GROUP // 2)
    def _(i):
        at = pl.ds(pl.multiple_of(i * 128, 128), 128)
        signal = (key[:, at].astype(F32) * value[:, at].astype(F32)).astype(BF16)
        mixed[:, at] = signal
        signal = signal.astype(F32)
        lags = taps[:, at].astype(F32)
        send_u[2 * i] = jnp.where(low_half, signal, pltpu.roll(lags, 64, 1)).astype(BF16)
        send_u[2 * i + 1] = jnp.where(low_half, pltpu.roll(signal, 64, 1), lags).astype(BF16)

    for copy in own[3:]:
        copy.start()

    def exchange(src, dst, send_sem, recv_sem):
        def one(k):
            peer = lax.rem(ctx + k, GROUP)
            return pltpu.make_async_remote_copy(
                src_ref=src.at[peer], dst_ref=dst.at[ctx],
                send_sem=send_sem.at[peer], recv_sem=recv_sem.at[ctx],
                device_id={"ctx": peer}, device_id_type=MESH)

        def arrival(k):
            peer = lax.rem(ctx + k, GROUP)
            return pltpu.make_async_remote_copy(
                src_ref=src.at[peer], dst_ref=dst.at[peer],
                send_sem=send_sem.at[peer], recv_sem=recv_sem.at[peer],
                device_id={"ctx": peer}, device_id_type=MESH)

        def start():
            @pl.loop(1, GROUP)
            def _(k):
                one(k).start()

        def wait_recv():
            @pl.loop(1, GROUP)
            def _(k):
                arrival(k).wait_recv()

        def wait_send():
            @pl.loop(1, GROUP)
            def _(k):
                one(k).wait_send()

        return start, wait_recv, wait_send

    u_start, u_wait, u_drain = exchange(send_u, recv_u, u_send, u_recv)
    c_start, c_wait, c_drain = exchange(send_c, recv_c, c_send, c_recv)
    u_start()
    recv_u[ctx] = send_u[ctx]

    def convolve():
        u_wait()
        loads["high"].wait()
        loads["low"].wait()

        @pl.loop(0, 4)
        def _(i):
            pair = jnp.concatenate(
                (recv_u[pl.ds(4 * i, 2)].reshape(BLOCK, 128),
                 recv_u[pl.ds(4 * i + 2, 2)].reshape(BLOCK, 128)), axis=1)
            result = jnp.dot(high[...], pair, preferred_element_type=F32)
            result += jnp.dot(low[...], pair, preferred_element_type=F32)
            for h in range(2):
                half = result[:, 128 * h:128 * h + 128]
                spec[2 * i + h] = half
                turned[2 * i + h] = pltpu.roll(half, 64, 1)

        @pl.loop(0, 16)
        def _(r):
            re = pl.ds(pl.multiple_of(16 * r, 16), 16)
            im = pl.ds(pl.multiple_of(BLOCK + 16 * r, 16), 16)
            sign = 1.0 - 2.0 * lax.div(r, 8).astype(F32)
            last = None
            for i in range(8):
                total_re = total_im = None
                for a in range(i // 2 + 1):
                    b = i - a
                    a_re, a_im = spec[a, re], spec[a, im]
                    b_re, b_im = turned[b, re], turned[b, im]
                    one_re = a_re * b_re - a_im * b_im
                    one_im = a_re * b_im + a_im * b_re
                    if a == b:
                        one_re, one_im = 0.5 * one_re, 0.5 * one_im
                    total_re = one_re if total_re is None else total_re + one_re
                    total_im = one_im if total_im is None else total_im + one_im
                if last is None:
                    joint[i, re] = total_re.astype(BF16)
                    joint[i, im] = total_im.astype(BF16)
                else:
                    joint[i, re] = (total_re - sign * last[1]).astype(BF16)
                    joint[i, im] = (total_im + sign * last[0]).astype(BF16)
                last = (total_re, total_im)

        loads["back"].wait()

        @pl.loop(0, 4)
        def _(i):
            pair = jnp.concatenate((joint[2 * i], joint[2 * i + 1]), axis=1)
            result = jnp.dot(back[...], pair, preferred_element_type=F32)
            for h in range(2):
                half = result[:, 128 * h:128 * h + 128]
                half = half + pltpu.roll(half, 64, 1)
                for d in range(2):
                    send_c[4 * i + 2 * h + d] = jnp.where(
                        low_half[:64], half[128 * d:128 * d + 64], half[128 * d + 64:128 * d + 128]
                    ).astype(BF16)


    weights = (wg, wu)
    offsets = (0, 3, 1, 2)

    def q_copy(g, by):
        peer = SIDE * g + turn(x, by)
        return pltpu.make_async_remote_copy(
            src_ref=send_q.at[g], dst_ref=recv_q.at[ctx],
            send_sem=q_send.at[peer], recv_sem=q_recv.at[ctx],
            device_id={"ctx": peer}, device_id_type=MESH)

    def prepare(k):
        g = turn(z, offsets[k])
        block = rows[pl.ds(2 * g, 2)].reshape(128, 512).astype(F32)
        squares = block * block
        squares = (squares[:, :128] + squares[:, 128:256]) + (
            squares[:, 256:384] + squares[:, 384:])
        send_q[g] = jnp.broadcast_to(jnp.sum(squares.T, axis=0, keepdims=True), (8, 128))
        scaled[k] = (block * gain_ref[...]).astype(BF16)
        for by in range(1, SIDE):
            q_copy(g, by).start()

        @pl.when(g != y)
        def _():
            q_copy(g, 0).start()

        @pl.when(g == y)
        def _():
            recv_q[ctx] = send_q[g]

    first = (x, y)
    second = (y, x)

    def partial(k, h, c):
        g = turn(z, offsets[k])
        part = parts[h][c]
        result = jnp.dot(
            scaled[k], weights[h][:, STARTS[c]:STARTS[c] + CHUNKS[c]],
            preferred_element_type=F32)
        for b in range(SIDE):
            if h == 0:
                part[b, g] = result[32 * b:32 * b + 32]
            else:
                part[g, b] = result[32 * b:32 * b + 32]

    def near(h, step, by):
        along_x = (h == 0) == (step == 0)
        return turn(x, by) + SIDE * y if along_x else x + SIDE * turn(y, by)

    last = n - 1

    def link(h, c, kind):
        if c == last and kind == 4:
            src, dst, by = t1_out[h][c], t0_in[h], 2
        else:
            src, dst, by = ends(h, c, kind)
        i = (h * n + c) * 8 + kind
        return pltpu.make_async_remote_copy(
            src_ref=src, dst_ref=dst, send_sem=r_send.at[i], recv_sem=r_recv.at[i],
            device_id={"ctx": near(h, 0 if kind < 4 else 1, by)}, device_id_type=MESH)

    def ends(h, c, kind):
        return (
            (s1_out[h][c].at[pl.ds(0, 2)], s1p_in[h][c], 1),
            (s1_out[h][c].at[pl.ds(2, 2)], s1m_in[h][c], 3),
            (s2p_out[h][c], s2p_in[h][c], 1),
            (s2m_out[h][c], s2m_in[h][c], 3),
            (t1_out[h][c].at[pl.ds(0, 16)], t1p_in[h][c], 1),
            (t1_out[h][c].at[pl.ds(16, 16)], t1m_in[h][c], 3),
            (t2p_out[h][c], t2p_in[h][c], 1),
            (t2m_out[h][c], t2m_in[h][c], 3),
        )[kind]

    top, bottom = pl.ds(0, 16), pl.ds(16, 16)

    def step1(h, c):
        s1_out[h][c][...] = parts[h][c][turn(first[h], 2)].astype(BF16)
        link(h, c, 0).start()
        link(h, c, 1).start()

    def step2(h, c):
        part, ahead, behind = parts[h][c], turn(first[h], 1), turn(first[h], 3)
        link(h, c, 0).wait_recv()
        for b in range(2):
            s2p_out[h][c][b] = (part[ahead, b] + s1p_in[h][c][b].astype(F32)).astype(BF16)
            s2p_out[h][c][2 + b] = part[ahead, 2 + b].astype(BF16)
        link(h, c, 2).start()
        link(h, c, 1).wait_recv()
        for b in range(2):
            s2m_out[h][c][b] = part[behind, b].astype(BF16)
            s2m_out[h][c][2 + b] = (
                part[behind, 2 + b] + s1m_in[h][c][b].astype(F32)).astype(BF16)
        link(h, c, 3).start()

    def step3(h, c):
        part, f, s = parts[h][c], first[h], second[h]
        link(h, c, 2).wait_recv()
        link(h, c, 3).wait_recv()
        for b in range(SIDE):
            part[f, b] = (
                part[f, b] + s2p_in[h][c][b].astype(F32) + s2m_in[h][c][b].astype(F32))
        t1_out[h][c][...] = part[f, turn(s, 2)].astype(BF16)
        link(h, c, 4).start()
        if c == last:
            t2p_out[h][c][...] = part[f, turn(s, 1)].astype(BF16)
            link(h, c, 6).start()
            t2m_out[h][c][...] = part[f, turn(s, 3)].astype(BF16)
            link(h, c, 7).start()
        else:
            link(h, c, 5).start()

    def step4(h, c):
        part, f, s = parts[h][c], first[h], second[h]
        ahead, behind = turn(s, 1), turn(s, 3)
        link(h, c, 4).wait_recv()
        t2p_out[h][c][top] = (part[f, ahead, top] + t1p_in[h][c][...].astype(F32)).astype(BF16)
        t2p_out[h][c][bottom] = part[f, ahead, bottom].astype(BF16)
        link(h, c, 6).start()
        link(h, c, 5).wait_recv()
        t2m_out[h][c][top] = part[f, behind, top].astype(BF16)
        t2m_out[h][c][bottom] = (
            part[f, behind, bottom] + t1m_in[h][c][...].astype(F32)).astype(BF16)
        link(h, c, 7).start()

    def finish(c, scale):
        at = slice(STARTS[c], STARTS[c] + CHUNKS[c])
        for h, out in enumerate((gate_ref, up_ref)):
            total = parts[h][c][first[h], second[h]]
            link(h, c, 6).wait_recv()
            total += t2p_in[h][c][...].astype(F32)
            link(h, c, 7).wait_recv()
            total += t2m_in[h][c][...].astype(F32)
            if c == last:
                link(h, c, 4).wait_recv()
                total += t0_in[h][...].astype(F32)
            out[:, at] = total * scale

    def multiply(k):
        for c in range(n):
            for h in range(2):
                partial(k, h, c)

    mate = 1 - core
    before, after, across = (turn(z, by) * 2 + mate for by in (3, 1, 2))
    loads["acts"].wait()
    z_copy(4, other, 0, other, whole=True).wait_recv()
    prepare(0)
    loads["wg"].wait()
    loads["wu"].wait()
    multiply(0)

    passed = []

    def forward(*copies):
        for copy in copies:
            copy.start()
            passed.append(copy)

    z_copy(0, left, 0, right).wait_recv()
    forward(z_copy(5, left, 0, right), z_copy(11, left, 0, right_mate))
    z_copy(1, right, 1, left).wait_recv()
    forward(z_copy(6, right, 1, left), z_copy(12, right, 1, left_mate))
    z_copy(2, left, 1, right).wait_recv()
    forward(z_copy(7, left, 0, other, whole=True))
    z_copy(3, right, 0, left).wait_recv()
    forward(z_copy(8, right, 0, other, whole=True))
    convolve()
    c_start()
    recv_c[ctx] = send_c[ctx]
    z_copy(7, before, 0, other, whole=True).wait_recv()
    prepare(1)
    multiply(1)
    z_copy(8, after, 0, other, whole=True).wait_recv()
    prepare(2)
    multiply(2)
    z_copy(5, far, 0, right).wait_recv()
    z_copy(6, far, 1, left).wait_recv()
    z_copy(11, across, 0, right_mate).wait_recv()
    z_copy(12, across, 1, left_mate).wait_recv()
    prepare(3)
    for c in range(n):
        for h in range(2):
            partial(3, h, c)
            step1(h, c)

    scale = None
    for c in range(n + 3):
        if c < n:
            step2(0, c)
            step2(1, c)
        if 0 <= c - 1 < n:
            step3(0, c - 1)
            step3(1, c - 1)
        if 0 <= c - 2 < last:
            step4(0, c - 2)
            step4(1, c - 2)
        if c == 0:
            for copy in own + passed:
                copy.wait_send()
            u_drain()
        if c == 1:
            c_wait()
            loads["query"].wait()
            direct_gain = skip_ref[...].astype(F32)
            for i in range(GROUP // 2):
                at = slice(128 * i, 128 * i + 128)
                even = recv_c[2 * i].astype(F32)
                odd = recv_c[2 * i + 1].astype(F32)
                conv = jnp.concatenate(
                    (jnp.where(low_half[:64], even, pltpu.roll(odd, 64, 1)),
                     jnp.where(low_half[:64], pltpu.roll(even, 64, 1), odd)), axis=0)
                direct = direct_gain[at].reshape(1, 128) * mixed[:, at].astype(F32)
                gated_ref[:, at] = (
                    query[:, at].astype(F32) * (conv + direct)).astype(BF16)
            c_drain()
        if c == 2:
            @pl.loop(1, GROUP)
            def _(i):
                peer = lax.rem(ctx + i, GROUP)
                pltpu.make_async_remote_copy(
                    src_ref=send_q.at[0], dst_ref=recv_q.at[peer],
                    send_sem=q_send.at[peer], recv_sem=q_recv.at[peer],
                    device_id={"ctx": peer}, device_id_type=MESH).wait_recv()

            power = recv_q[0]
            for i in range(1, GROUP):
                power = power + recv_q[i]
            spread[...] = jnp.broadcast_to(power[0:1], (128, 128)).T
            mine = spread[pl.ds(pl.multiple_of(32 * x, 32), 32), :]
            scale = lax.rsqrt(mine[:, :1] / D + EPSILON)
            for k in range(SIDE):
                g = turn(z, offsets[k])
                for by in range(1, SIDE):
                    q_copy(g, by).wait_send()

                @pl.when(g != y)
                def _(g=g):
                    q_copy(g, 0).wait_send()
        if c >= 3:
            finish(c - 3, scale)
            for h in range(2):
                for kind in range(8):
                    if c - 3 != last or kind != 5:
                        link(h, c - 3, kind).wait_send()


def body(query_b, key_b, value_b, filter_b, skip_b, acts_a, gain_a, w_gate, w_up, grad_hidden):
    high, low, back = dft_tables()
    any_spec = pl.BlockSpec(memory_space=pl.ANY)
    vmem = pl.BlockSpec(memory_space=pltpu.VMEM)
    length, width = key_b.shape
    hidden = w_gate.shape[1]

    def per_chunk(*lead, kind=BF16):
        return [pltpu.VMEM(lead + (w,), kind) for w in CHUNKS] * 2

    scratch = [
        pltpu.VMEM((length, width), BF16),
        pltpu.VMEM((length, width), BF16),
        pltpu.VMEM((length, width), BF16),
        pltpu.VMEM((length, width), BF16),
        pltpu.VMEM(w_gate.shape, BF16),
        pltpu.VMEM(w_up.shape, BF16),
        pltpu.VMEM(high.shape, BF16),
        pltpu.VMEM(low.shape, BF16),
        pltpu.VMEM(back.shape, BF16),
        pltpu.VMEM((length, width), BF16),
        pltpu.VMEM((GROUP, 128, 128), BF16),
        pltpu.VMEM((GROUP, 128, 128), BF16),
        pltpu.VMEM((8, 2 * BLOCK, 128), F32),
        pltpu.VMEM((8, 2 * BLOCK, 128), F32),
        pltpu.VMEM((8, 2 * BLOCK, 128), BF16),
        pltpu.VMEM((GROUP, 64, 128), BF16),
        pltpu.VMEM((GROUP, 64, 128), BF16),
        pltpu.VMEM((8, 64, 512), BF16),
        pltpu.VMEM((SIDE, 128, 512), BF16),
        pltpu.VMEM((SIDE, 8, 128), F32),
        pltpu.VMEM((GROUP, 8, 128), F32),
        pltpu.VMEM((128, 128), F32),
    ]
    scratch += per_chunk(SIDE, SIDE, 32, kind=F32)
    for lead in (
        (SIDE, 32), (2, 32), (2, 32), (SIDE, 32), (SIDE, 32), (SIDE, 32), (SIDE, 32),
        (32,), (16,), (16,), (32,), (32,), (32,), (32,),
    ):
        scratch += per_chunk(*lead)
    scratch += [pltpu.VMEM((32, CHUNKS[-1]), BF16)] * 2
    links = 2 * len(CHUNKS) * 8
    for size in (10, GROUP, GROUP, GROUP, GROUP, GROUP, GROUP, 13, 13, links, links):
        scratch.append(pltpu.SemaphoreType.DMA((size,)))
    gated, gate, up = pl.pallas_call(
        kernel,
        out_shape=(
            pltpu.VMEM((length, width), BF16),
            pltpu.VMEM(grad_hidden.shape, F32),
            pltpu.VMEM(grad_hidden.shape, F32),
        ),
        in_specs=[any_spec] * 4 + [vmem, any_spec, vmem] + [any_spec] * 5,
        out_specs=(vmem, vmem, vmem),
        scratch_shapes=scratch,
        compiler_params=pltpu.CompilerParams(
            collective_id=0, has_side_effects=True, vmem_limit_bytes=56 * 1024 * 1024),
        name="hyena",
    )(
        query_b, key_b, value_b, filter_b, skip_b, acts_a,
        gain_a.reshape(1, -1), w_gate, w_up,
        jnp.asarray(high), jnp.asarray(low), jnp.asarray(back),
    )
    sigma = jax.nn.sigmoid(gate)
    upstream = grad_hidden.astype(F32)
    grad_gate = (upstream * up * sigma * (1.0 + gate * (1.0 - sigma))).astype(BF16)
    grad_up = (upstream * gate * sigma).astype(BF16)
    return gated, grad_gate, grad_up


def solution(mesh):
    return jax.shard_map(
        body,
        mesh=mesh,
        in_specs=(
            P(("dp", "ctx"), "tp"),
            P(("dp", "ctx"), "tp"),
            P(("dp", "ctx"), "tp"),
            P("ctx", "tp"),
            P("tp"),
            P(("dp", "tp"), "ctx"),
            P("ctx"),
            P("ctx", "tp"),
            P("ctx", "tp"),
            P(("dp", "ctx"), "tp"),
        ),
        out_specs=(P(("dp", "ctx"), "tp"), P(("dp", "ctx"), "tp"), P(("dp", "ctx"), "tp")),
        check_vma=False,
    )
```

time: 182 us -> 58.2 us (0.32)
  the two profiles are of different devices: /device:TPU:1 before, /device:TPU:32 now
where the time goes in v2:
time: 58.2 us; the launch traced here: 58.1 us
  Pallas kernels  55.9 us (96%)
  other arithmetic  0.76 us (1%)
  local copies, waits for them, and re-layouts  0.71 us (1%)
  between operations  0.66 us (1%)
    pallas_call x1, Pallas kernels, body(): pl.pallas_call(kernel, out_shape=(pltpu.VMEM((length, width), BF16), pltp...  55.9 us

profile of v2, /device:TPU:32, one launch (start us, length us, event | category | flops | bytes accessed | tf_op | source)
XLA Modules:
  0.0 58.1 jit_solution(16029175566861536821)
XLA Ops:
  0.6 0.0 copy-start
  0.6 55.9 %hyena.1 = (bf16[128,1024]{1,0:T(8,128)(2,1)S(1)}, f32[32,1408]{1,0:T(8,128)S(1)}, f32[32,1408]{1,0:T(8,128)S(1)}) custom-call(bf16[128,1024]{1,0:T(8,128)(2,1)} %query_h.1, bf16[128,1024]{1,0:T(8,128)(2,1)} %key_h.1, bf16[128,1024]{1,0:T(8,128)(2,1)} %value_h.1, bf16[128,1024]{1,0:T(8,128)(2,1)} %taps_h.1, bf16[1024]{0:T(1024)(128)(2,1)} %skip_ref.1, ...), custom_call_target="tpu_custom_call" | custom-call | tf_op jit(solution)/shard_map/hyena/pallas_call | solution.py:508
  56.6 0.0 copy-done
  56.6 0.8 %fusion.4 = (bf16[32,1408]{1,0:T(8,128)(2,1)}, bf16[32,1408]{1,0:T(8,128)(2,1)}) fusion(f32[32,1408]{1,0:T(8,128)S(1)} %get-tuple-element.8, bf16[32,1408]{1,0:T(8,128)(2,1)S(1)} %copy-done, f32[32,1408]{1,0:T(8,128)S(1)} %get-tuple-element.7), kind=kLoop, calls=%fused_computation.6 | loop fusion | flops 630784 | bytes 630784 | tf_op jit(solution)/shard_map/convert_element_type | solution.py:529
  57.4 0.7 %copy.17 = bf16[128,1024]{1,0:T(8,128)(2,1)} copy(bf16[128,1024]{1,0:T(8,128)(2,1)S(1)} %get-tuple-element.11) | data formatting | bytes 524288
Async XLA Ops:
  0.6 56.0 %copy-start = (bf16[32,1408]{1,0:T(8,128)(2,1)S(1)}, bf16[32,1408]{1,0:T(8,128)(2,1)}, u32[]{:S(2)}) copy-start(bf16[32,1408]{1,0:T(8,128)(2,1)} %param.22) | copy-start | bytes 270340

commit v3 on v2

--- a/solution.py
+++ b/solution.py
@@ -13,7 +13,7 @@
 SIDE = 4
 GROUP = 16
 BLOCK = 256
-CHUNKS = (384, 384, 384, 256)
+CHUNKS = (768, 640)
 STARTS = tuple(sum(CHUNKS[:i]) for i in range(len(CHUNKS)))
 MESH = pl.DeviceIdType.MESH
 F32 = jnp.float32
@@ -46,9 +46,9 @@
         (rest[2 * i * n:(2 * i + 1) * n], rest[(2 * i + 1) * n:(2 * i + 2) * n])
         for i in range(15)
     )
-    t0_in = rest[30 * n:30 * n + 2]
+    t0_in = (rest[30 * n:31 * n], rest[31 * n:32 * n])
     (load_sem, u_send, u_recv, c_send, c_recv, q_send, q_recv, z_send, z_recv,
-     r_send, r_recv) = rest[30 * n + 2:]
+     r_send, r_recv) = rest[32 * n:]
 
     ctx = lax.axis_index("ctx")
     tp = lax.axis_index("tp")
@@ -118,8 +118,6 @@
         send_u[2 * i] = jnp.where(low_half, signal, pltpu.roll(lags, 64, 1)).astype(BF16)
         send_u[2 * i + 1] = jnp.where(low_half, pltpu.roll(signal, 64, 1), lags).astype(BF16)
 
-    for copy in own[3:]:
-        copy.start()
 
     def exchange(src, dst, send_sem, recv_sem):
         def one(k):
@@ -157,6 +155,8 @@
     c_start, c_wait, c_drain = exchange(send_c, recv_c, c_send, c_recv)
     u_start()
     recv_u[ctx] = send_u[ctx]
+    for copy in own[3:]:
+        copy.start()
 
     def convolve():
         u_wait()
@@ -229,11 +229,15 @@
     def prepare(k):
         g = turn(z, offsets[k])
         block = rows[pl.ds(2 * g, 2)].reshape(128, 512).astype(F32)
+        scaled[k] = (block * gain_ref[...]).astype(BF16)
+
+    def squares_of(k):
+        g = turn(z, offsets[k])
+        block = rows[pl.ds(2 * g, 2)].reshape(128, 512).astype(F32)
         squares = block * block
         squares = (squares[:, :128] + squares[:, 128:256]) + (
             squares[:, 256:384] + squares[:, 384:])
         send_q[g] = jnp.broadcast_to(jnp.sum(squares.T, axis=0, keepdims=True), (8, 128))
-        scaled[k] = (block * gain_ref[...]).astype(BF16)
         for by in range(1, SIDE):
             q_copy(g, by).start()
 
@@ -267,8 +271,8 @@
     last = n - 1
 
     def link(h, c, kind):
-        if c == last and kind == 4:
-            src, dst, by = t1_out[h][c], t0_in[h], 2
+        if kind == 4:
+            src, dst, by = t1_out[h][c], t0_in[h][c], 2
         else:
             src, dst, by = ends(h, c, kind)
         i = (h * n + c) * 8 + kind
@@ -318,13 +322,10 @@
                 part[f, b] + s2p_in[h][c][b].astype(F32) + s2m_in[h][c][b].astype(F32))
         t1_out[h][c][...] = part[f, turn(s, 2)].astype(BF16)
         link(h, c, 4).start()
-        if c == last:
-            t2p_out[h][c][...] = part[f, turn(s, 1)].astype(BF16)
-            link(h, c, 6).start()
-            t2m_out[h][c][...] = part[f, turn(s, 3)].astype(BF16)
-            link(h, c, 7).start()
-        else:
-            link(h, c, 5).start()
+        t2p_out[h][c][...] = part[f, turn(s, 1)].astype(BF16)
+        link(h, c, 6).start()
+        t2m_out[h][c][...] = part[f, turn(s, 3)].astype(BF16)
+        link(h, c, 7).start()
 
     def step4(h, c):
         part, f, s = parts[h][c], first[h], second[h]
@@ -347,9 +348,9 @@
             total += t2p_in[h][c][...].astype(F32)
             link(h, c, 7).wait_recv()
             total += t2m_in[h][c][...].astype(F32)
-            if c == last:
+            if True:
                 link(h, c, 4).wait_recv()
-                total += t0_in[h][...].astype(F32)
+                total += t0_in[h][c][...].astype(F32)
             out[:, at] = total * scale
 
     def multiply(k):
@@ -362,6 +363,7 @@
     loads["acts"].wait()
     z_copy(4, other, 0, other, whole=True).wait_recv()
     prepare(0)
+    squares_of(0)
     loads["wg"].wait()
     loads["wu"].wait()
     multiply(0)
@@ -386,29 +388,43 @@
     recv_c[ctx] = send_c[ctx]
     z_copy(7, before, 0, other, whole=True).wait_recv()
     prepare(1)
+    squares_of(1)
     multiply(1)
     z_copy(8, after, 0, other, whole=True).wait_recv()
     prepare(2)
+    squares_of(2)
     multiply(2)
+
+    @pl.when(y != z)
+    def _():
+        for c in range(n):
+            step1(1, c)
+
     z_copy(5, far, 0, right).wait_recv()
     z_copy(6, far, 1, left).wait_recv()
     z_copy(11, across, 0, right_mate).wait_recv()
     z_copy(12, across, 1, left_mate).wait_recv()
     prepare(3)
     for c in range(n):
-        for h in range(2):
-            partial(3, h, c)
-            step1(h, c)
+        partial(3, 0, c)
+        step1(0, c)
+        partial(3, 1, c)
+
+        @pl.when(y == z)
+        def _(c=c):
+            step1(1, c)
+
+    squares_of(3)
 
     scale = None
-    for c in range(n + 3):
+    for c in range(n + 2):
         if c < n:
             step2(0, c)
             step2(1, c)
         if 0 <= c - 1 < n:
             step3(0, c - 1)
             step3(1, c - 1)
-        if 0 <= c - 2 < last:
+        if False:
             step4(0, c - 2)
             step4(1, c - 2)
         if c == 0:
@@ -453,12 +469,12 @@
                 @pl.when(g != y)
                 def _(g=g):
                     q_copy(g, 0).wait_send()
-        if c >= 3:
-            finish(c - 3, scale)
+        if c >= 2:
+            finish(c - 2, scale)
             for h in range(2):
                 for kind in range(8):
-                    if c - 3 != last or kind != 5:
-                        link(h, c - 3, kind).wait_send()
+                    if kind != 5:
+                        link(h, c - 2, kind).wait_send()
 
 
 def body(query_b, key_b, value_b, filter_b, skip_b, acts_a, gain_a, w_gate, w_up, grad_hidden):
@@ -501,7 +517,7 @@
         (32,), (16,), (16,), (32,), (32,), (32,), (32,),
     ):
         scratch += per_chunk(*lead)
-    scratch += [pltpu.VMEM((32, CHUNKS[-1]), BF16)] * 2
+    scratch += per_chunk(32)
     links = 2 * len(CHUNKS) * 8
     for size in (10, GROUP, GROUP, GROUP, GROUP, GROUP, GROUP, 13, 13, links, links):
         scratch.append(pltpu.SemaphoreType.DMA((size,)))

time: 58.2 us -> 55.4 us (0.952)
  the two profiles are of different devices: /device:TPU:32 before, /device:TPU:1 now
where the time goes in v3:
time: 55.4 us; the launch traced here: 54.5 us
  Pallas kernels  52.4 us (95%)
  other arithmetic  0.76 us (1%)
  local copies, waits for them, and re-layouts  0.71 us (1%)
  between operations  0.66 us (1%)
    pallas_call x1, Pallas kernels, body(): pl.pallas_call(kernel, out_shape=(pltpu.VMEM((length, width), BF16), pltp...  52.4 us

profile of v3, /device:TPU:1, one launch (start us, length us, event | category | flops | bytes accessed | tf_op | source)
XLA Modules:
  0.0 54.5 jit_solution(8149449408688225750)
XLA Ops:
  0.6 0.0 copy-start
  0.6 52.4 %hyena.1 = (bf16[128,1024]{1,0:T(8,128)(2,1)S(1)}, f32[32,1408]{1,0:T(8,128)S(1)}, f32[32,1408]{1,0:T(8,128)S(1)}) custom-call(bf16[128,1024]{1,0:T(8,128)(2,1)} %query_h.1, bf16[128,1024]{1,0:T(8,128)(2,1)} %key_h.1, bf16[128,1024]{1,0:T(8,128)(2,1)} %value_h.1, bf16[128,1024]{1,0:T(8,128)(2,1)} %taps_h.1, bf16[1024]{0:T(1024)(128)(2,1)} %skip_ref.1, ...), custom_call_target="tpu_custom_call" | custom-call | tf_op jit(solution)/shard_map/hyena/pallas_call | solution.py:524
  53.0 0.0 copy-done
  53.1 0.8 %fusion.4 = (bf16[32,1408]{1,0:T(8,128)(2,1)}, bf16[32,1408]{1,0:T(8,128)(2,1)}) fusion(f32[32,1408]{1,0:T(8,128)S(1)} %get-tuple-element.8, bf16[32,1408]{1,0:T(8,128)(2,1)S(1)} %copy-done, f32[32,1408]{1,0:T(8,128)S(1)} %get-tuple-element.7), kind=kLoop, calls=%fused_computation.6 | loop fusion | flops 630784 | bytes 630784 | tf_op jit(solution)/shard_map/convert_element_type | solution.py:545
  53.8 0.7 %copy.17 = bf16[128,1024]{1,0:T(8,128)(2,1)} copy(bf16[128,1024]{1,0:T(8,128)(2,1)S(1)} %get-tuple-element.11) | data formatting | bytes 524288
Async XLA Ops:
  0.6 52.4 %copy-start = (bf16[32,1408]{1,0:T(8,128)(2,1)S(1)}, bf16[32,1408]{1,0:T(8,128)(2,1)}, u32[]{:S(2)}) copy-start(bf16[32,1408]{1,0:T(8,128)(2,1)} %param.22) | copy-start | bytes 270340

commit v4 on v3

--- a/solution.py
+++ b/solution.py
@@ -2,7 +2,6 @@
 
 import jax
 import jax.numpy as jnp
-import numpy as np
 from jax import lax
 from jax.experimental import pallas as pl
 from jax.experimental.pallas import tpu as pltpu
@@ -20,20 +19,28 @@
 BF16 = jnp.bfloat16
 
 
-def dft_tables():
-    order = np.concatenate((np.arange(0, BLOCK, 2), np.arange(1, BLOCK, 2)))
-    angle = np.outer(2 * order + 1, np.arange(BLOCK)) % (4 * BLOCK)
-    angle = angle.astype(np.float64) * (math.pi / (2 * BLOCK))
-    full = np.concatenate((np.cos(angle), -np.sin(angle)), axis=0)
-    high = full.astype(jnp.bfloat16)
-    low = (full - high.astype(np.float64)).astype(jnp.bfloat16)
-    back = np.ascontiguousarray((full.T / BLOCK)).astype(jnp.bfloat16)
-    return high, low, back
+def fill_tables(high, low, back):
+    half = BLOCK // 2
+
+    @pl.loop(0, BLOCK // 16)
+    def _(i):
+        row = lax.broadcasted_iota(jnp.int32, (16, BLOCK), 0) + 16 * i
+        order = 2 * row - jnp.where(row >= half, BLOCK - 1, 0)
+        turns = (2 * order + 1) * lax.broadcasted_iota(jnp.int32, (16, BLOCK), 1)
+        turns = lax.rem(turns, 4 * BLOCK)
+        turns = jnp.where(turns > 2 * BLOCK, turns - 4 * BLOCK, turns)
+        angle = turns.astype(F32) * (math.pi / (2 * BLOCK))
+        for start, value in ((0, jnp.cos(angle)), (BLOCK, -jnp.sin(angle))):
+            at = pl.ds(pl.multiple_of(start + 16 * i, 16), 16)
+            rounded = value.astype(BF16)
+            high[at] = rounded
+            low[at] = (value - rounded.astype(F32)).astype(BF16)
+
+    back[...] = (high[...].astype(F32).T * (1.0 / BLOCK)).astype(BF16)
 
 
 def kernel(
     query_h, key_h, value_h, taps_h, skip_ref, acts_h, gain_ref, wg_h, wu_h,
-    high_h, low_h, back_h,
     gated_ref, gate_ref, up_ref,
     query, key, value, taps, wg, wu, high, low, back,
     mixed, send_u, recv_u, spec, turned, joint, send_c, recv_c,
@@ -77,8 +84,8 @@
     loads = {}
     for i, (name, src, dst) in enumerate((
         ("key", key_h, key), ("value", value_h, value), ("taps", taps_h, taps),
-        ("acts", acts_h, rows.at[tp]), ("high", high_h, high), ("low", low_h, low),
-        ("wg", wg_h, wg), ("wu", wu_h, wu), ("back", back_h, back),
+        ("acts", acts_h, rows.at[tp]),
+        ("wg", wg_h, wg), ("wu", wu_h, wu),
         ("query", query_h, query),
     )):
         loads[name] = pltpu.make_async_copy(src, dst, load_sem.at[i])
@@ -160,8 +167,6 @@
 
     def convolve():
         u_wait()
-        loads["high"].wait()
-        loads["low"].wait()
 
         @pl.loop(0, 4)
         def _(i):
@@ -201,7 +206,6 @@
                     joint[i, im] = (total_im + sign * last[0]).astype(BF16)
                 last = (total_re, total_im)
 
-        loads["back"].wait()
 
         @pl.loop(0, 4)
         def _(i):
@@ -360,6 +364,7 @@
 
     mate = 1 - core
     before, after, across = (turn(z, by) * 2 + mate for by in (3, 1, 2))
+    fill_tables(high, low, back)
     loads["acts"].wait()
     z_copy(4, other, 0, other, whole=True).wait_recv()
     prepare(0)
@@ -478,7 +483,6 @@
 
 
 def body(query_b, key_b, value_b, filter_b, skip_b, acts_a, gain_a, w_gate, w_up, grad_hidden):
-    high, low, back = dft_tables()
     any_spec = pl.BlockSpec(memory_space=pl.ANY)
     vmem = pl.BlockSpec(memory_space=pltpu.VMEM)
     length, width = key_b.shape
@@ -494,9 +498,9 @@
         pltpu.VMEM((length, width), BF16),
         pltpu.VMEM(w_gate.shape, BF16),
         pltpu.VMEM(w_up.shape, BF16),
-        pltpu.VMEM(high.shape, BF16),
-        pltpu.VMEM(low.shape, BF16),
-        pltpu.VMEM(back.shape, BF16),
+        pltpu.VMEM((2 * BLOCK, BLOCK), BF16),
+        pltpu.VMEM((2 * BLOCK, BLOCK), BF16),
+        pltpu.VMEM((BLOCK, 2 * BLOCK), BF16),
         pltpu.VMEM((length, width), BF16),
         pltpu.VMEM((GROUP, 128, 128), BF16),
         pltpu.VMEM((GROUP, 128, 128), BF16),
@@ -528,7 +532,7 @@
             pltpu.VMEM(grad_hidden.shape, F32),
             pltpu.VMEM(grad_hidden.shape, F32),
         ),
-        in_specs=[any_spec] * 4 + [vmem, any_spec, vmem] + [any_spec] * 5,
+        in_specs=[any_spec] * 4 + [vmem, any_spec, vmem] + [any_spec] * 2,
         out_specs=(vmem, vmem, vmem),
         scratch_shapes=scratch,
         compiler_params=pltpu.CompilerParams(
@@ -537,7 +541,6 @@
     )(
         query_b, key_b, value_b, filter_b, skip_b, acts_a,
         gain_a.reshape(1, -1), w_gate, w_up,
-        jnp.asarray(high), jnp.asarray(low), jnp.asarray(back),
     )
     sigma = jax.nn.sigmoid(gate)
     upstream = grad_hidden.astype(F32)

time: 55.4 us -> 55.1 us (level)
  the two profiles are of different devices: /device:TPU:1 before, /device:TPU:8 now
where the time goes in v4:
time: 55.1 us; the launch traced here: 54.9 us
  Pallas kernels  52.8 us (96%)
  other arithmetic  0.76 us (1%)
  local copies, waits for them, and re-layouts  0.71 us (1%)
  between operations  0.66 us (1%)
    pallas_call x1, Pallas kernels, body(): pl.pallas_call(kernel, out_shape=(pltpu.VMEM((length, width), BF16), pltp...  52.8 us

profile of v4, /device:TPU:8, one launch (start us, length us, event | category | flops | bytes accessed | tf_op | source)
XLA Modules:
  0.0 54.9 jit_solution(12481400227682923207)
XLA Ops:
  0.6 0.0 copy-start
  0.6 52.8 %hyena.1 = (bf16[128,1024]{1,0:T(8,128)(2,1)S(1)}, f32[32,1408]{1,0:T(8,128)S(1)}, f32[32,1408]{1,0:T(8,128)S(1)}) custom-call(bf16[128,1024]{1,0:T(8,128)(2,1)} %query_h.1, bf16[128,1024]{1,0:T(8,128)(2,1)} %key_h.1, bf16[128,1024]{1,0:T(8,128)(2,1)} %value_h.1, bf16[128,1024]{1,0:T(8,128)(2,1)} %taps_h.1, bf16[1024]{0:T(1024)(128)(2,1)} %skip_ref.1, ...), custom_call_target="tpu_custom_call" | custom-call | tf_op jit(solution)/shard_map/hyena/pallas_call | solution.py:528
  53.5 0.0 copy-done
  53.5 0.8 %fusion.4 = (bf16[32,1408]{1,0:T(8,128)(2,1)}, bf16[32,1408]{1,0:T(8,128)(2,1)}) fusion(f32[32,1408]{1,0:T(8,128)S(1)} %get-tuple-element.8, bf16[32,1408]{1,0:T(8,128)(2,1)S(1)} %copy-done, f32[32,1408]{1,0:T(8,128)S(1)} %get-tuple-element.7), kind=kLoop, calls=%fused_computation.6 | loop fusion | flops 630784 | bytes 630784 | tf_op jit(solution)/shard_map/convert_element_type | solution.py:548
  54.2 0.7 %copy.14 = bf16[128,1024]{1,0:T(8,128)(2,1)} copy(bf16[128,1024]{1,0:T(8,128)(2,1)S(1)} %get-tuple-element.11) | data formatting | bytes 524288
Async XLA Ops:
  0.6 52.8 %copy-start = (bf16[32,1408]{1,0:T(8,128)(2,1)S(1)}, bf16[32,1408]{1,0:T(8,128)(2,1)}, u32[]{:S(2)}) copy-start(bf16[32,1408]{1,0:T(8,128)(2,1)} %param.19) | copy-start | bytes 270340
